TPU v7x, 128 devices: a whole 4x4x4 slice. The times are simulated.
128 devices in a mesh: row: 8 (over z, core), col: 16 (over x, y).
Axes of the slice: x: 4, y: 4, z: 4, core: 2. Of those that a mesh axis runs over, the one named last changes fastest.
Arguments:
- loaded: bfloat16 [8192, 4096], P(('row', 'col')), may hold values from -6 to 6
- lengths: int32 [128, 8], replicated, may hold values from 1 to 15, as said below
- offsets: int32 [128, 8], replicated, may hold values from 0 to 8191, as said below
- gate_weight: bfloat16 [4096, 14784], P(None, 'col'), may hold values from -0.09375 to 0.09375
- up_weight: bfloat16 [4096, 14784], P(None, 'col'), may hold values from -0.09375 to 0.09375
- down_weight: bfloat16 [14784, 4096], P('col'), may hold values from -0.046875 to 0.046875
Outputs:
- mixed: bfloat16 [8192, 4096], P('row', 'col')
Inputs may be any that keep to these rules, and one draw needn't show every extreme that they name: Each loader device's pieces 2q and 2q + 1 have lengths summing to 16. `offsets`: every packed position receives exactly one token. The tokens of one loader device that land in one row block of 1024 positions number either 0 or exactly 16; each loader device feeds exactly 4 row blocks.
All inputs are finite; a program needn't handle non-finite values.
Results may differ from a plain program's by a relative error of at most 0.0049.
Values may be sent and summed in bfloat16 or wider, within the bound.
A program may use at most 192 MiB of HBM per device.

v0:
```python
import jax
import jax.numpy as jnp
from jax import lax
from jax.sharding import PartitionSpec as P


def destinations(lengths, offsets, load_dev):
    ends = jnp.cumsum(lengths, axis=1)
    starts = ends - lengths
    positions = jnp.arange(load_dev, dtype=jnp.int32)
    which = jnp.sum((positions[None, :, None] >= ends[:, None, :]).astype(jnp.int32), axis=2)
    base = jnp.take_along_axis(offsets - starts, which, axis=1)
    return base + positions[None, :]


def slot_ranks(block_rows, n_row):
    marks = (block_rows[:, :, None] == jnp.arange(n_row, dtype=jnp.int32)[None, None, :]).astype(
        jnp.int32
    )
    before = jnp.cumsum(marks, axis=1) - marks
    return jnp.sum(before * marks, axis=2)


def per_device(loaded, lengths, offsets, gate_weight, up_weight, down_weight):
    n_row = lax.axis_size("row")
    n_col = lax.axis_size("col")
    load_dev = loaded.shape[0]
    width = loaded.shape[1]
    col_width = width // n_col
    capacity = load_dev // 4
    tok_row = load_dev * n_col
    sources = n_row * n_col
    position = destinations(lengths, offsets, load_dev)
    block_rows = position // tok_row
    slots = slot_ranks(block_rows, n_row)
    sender = lax.axis_index("row") * n_col + lax.axis_index("col")
    my_rows = lax.dynamic_index_in_dim(block_rows, sender, 0, keepdims=False)
    my_slots = lax.dynamic_index_in_dim(slots, sender, 0, keepdims=False)
    target = my_rows * capacity + my_slots
    select = (target[None, :] == jnp.arange(n_row * capacity, dtype=jnp.int32)[:, None]).astype(
        jnp.bfloat16
    )
    select = select.reshape(n_row, capacity, load_dev)
    outgoing = jnp.einsum(
        "rql,lcd->rcqd",
        select,
        loaded.reshape(load_dev, n_col, col_width),
        preferred_element_type=jnp.float32,
    ).astype(jnp.bfloat16)
    arrived = lax.all_to_all(
        outgoing.reshape(sources, capacity, col_width),
        ("row", "col"),
        split_axis=0,
        concat_axis=0,
        tiled=True,
    )
    arrived = arrived.reshape(sources * capacity, col_width)
    my_block = lax.axis_index("row")
    source_ids = jnp.arange(sources, dtype=jnp.int32)[:, None]
    flat_slot = source_ids * capacity + slots
    in_row = position % tok_row
    landing = jnp.where(block_rows == my_block, in_row, tok_row)
    lookup = (
        jnp.zeros((tok_row,), jnp.int32)
        .at[landing.reshape(-1)]
        .set(flat_slot.reshape(-1), mode="drop")
    )
    packed = jnp.take(arrived, lookup, axis=0)
    piece = lax.all_gather(packed, "col", axis=1, tiled=True)
    gate = jnp.dot(piece, gate_weight, preferred_element_type=jnp.float32)
    up = jnp.dot(piece, up_weight, preferred_element_type=jnp.float32)
    hidden = (jax.nn.silu(gate) * up).astype(jnp.bfloat16)
    partial_term = jnp.dot(hidden, down_weight, preferred_element_type=jnp.float32)
    mixed = lax.psum_scatter(partial_term, "col", scatter_dimension=1, tiled=True).astype(
        jnp.bfloat16
    )
    return mixed


def solution(mesh):
    placed = (P(("row", "col"), None), P(), P(), P(None, "col"), P(None, "col"), P("col", None))
    return jax.shard_map(
        per_device, mesh=mesh, in_specs=placed, out_specs=P("row", "col"), check_vma=False
    )
```

profile of v0, /device:TPU:1, one launch (start us, length us, event | category | flops | bytes accessed | tf_op | source)
XLA Modules:
  0.0 331.7 jit_solution(2242582135416691902)
XLA Ops:
  6.5 0.7 reduce_window_sum.22
  7.2 0.1 convert_reduce_fusion
  7.3 0.7 subtract_subtract_fusion
  8.1 0.1 copy.26
  8.2 0.1 reshape.242
  8.2 0.0 copy-start
  8.2 33.4 %gather_fusion.1 = s32[8192]{0:T(1024)S(1)} fusion(s32[128,8]{0,1:T(8,128)S(1)} %subtract_subtract_fusion, s32[8192]{0:T(1024)S(1)} %reshape.242), kind=kCustom, calls=%fused_computation.1 | custom fusion | bytes 131072 | tf_op jit(solution)/shard_map/jit(take_along_axis)/gather | solution.py:12
  41.6 0.1 reshape.245
  41.7 0.1 copy.27
  41.8 0.1 add_select_fusion
  41.8 0.1 fusion.20
  41.9 0.2 add_reduce_fusion
  42.1 0.0 copy-done
  42.1 1.5 convolution_convert_fusion
  43.6 11.5 %all-to-all-start = ((bf16[128,16,256]{2,1,0:T(8,128)(2,1)}), bf16[128,16,256]{2,1,0:T(8,128)(2,1)S(1)}, u32[]{:S(2)}, u32[]{:S(2)}) async-start(bf16[128,16,256]{2,1,0:T(8,128)(2,1)} %bitcast.7), calls=%async_computation | async-start | bytes 2097152 | tf_op jit(solution)/shard_map/all_to_all | solution.py:50
  55.1 0.0 all-gather.2.cloned.1.call-start
  55.1 0.1 copy.25
  55.2 0.1 reduce_sum.23
  55.4 0.1 add.147
  55.5 0.3 compare_select_fusion
  55.8 0.1 copy.28
  55.9 0.1 reshape.252
  56.0 30.4 %scatter_custom_fusion = s32[1024]{0:T(1024)S(1)} fusion(s32[8192]{0:T(1024)S(1)} %bitcast.31, s32[8192]{0:T(1024)S(1)} %reshape.252, s32[]{:T(128)} %constant.75.clone.1), kind=kCustom, calls=%fused_computation.51 | custom fusion | bytes 4100 | tf_op jit(solution)/shard_map/scatter | solution.py:66
  86.5 0.0 all-to-all-done
  86.5 3.9 %gather_fusion = bf16[1024,256]{1,0:T(8,128)(2,1)S(1)} fusion(bf16[2048,256]{1,0:T(8,128)(2,1)S(1)} %bitcast.28, s32[1024]{0:T(1024)S(1)} %fusion.16), kind=kCustom, calls=%fused_computation | custom fusion | bytes 1052672 | tf_op jit(solution)/shard_map/jit(_take)/gather | solution.py:68
  90.5 1.0 broadcast_select_fusion
  91.5 0.0 all-gather.2.cloned.1.call-update
  91.5 0.2 reduce-scatter.2.cloned.1.call-start
  91.7 78.7 %all-gather.2.cloned.1.call-done = bf16[1024,4096]{1,0:T(8,128)(2,1)} async-done(((bf16[1024,256]{1,0:T(8,128)(2,1)}), bf16[1024,4096]{1,0:T(8,128)(2,1)}) %all-gather.2.cloned.1.call-update) | async-done | bytes 8388624 | tf_op jit(solution)/shard_map/all_gather | solution.py:69
  170.5 14.0 %fusion.21 = f32[1024,924]{0,1:T(8,128)} fusion(bf16[1024,4096]{1,0:T(8,128)(2,1)} %all-gather.2.cloned.1.call-done, bf16[4096,924]{0,1:T(8,128)(2,1)} %param.9), kind=kOutput, calls=%fused_computation.56 | convolution fusion | flops 7751073792 | bytes 19742720 | tf_op jit(solution)/shard_map/dot_general | solution.py:70
  184.4 27.8 %fusion = f32[1024,4096]{1,0:T(8,128)} fusion(bf16[924,4096]{1,0:T(8,128)(2,1)} %param.11, f32[1024,924]{0,1:T(8,128)} %fusion.21, bf16[1024,4096]{1,0:T(8,128)(2,1)} %all-gather.2.cloned.1.call-done, bf16[4096,924]{0,1:T(8,128)(2,1)} %param.10), kind=kOutput, calls=%fused_computation.4 | convolution fusion | flops 15507824640 | bytes 44089344 | tf_op jit(solution)/shard_map/dot_general | solution.py:73
  212.2 0.0 reduce-scatter.2.cloned.1.call-update
  212.2 110.6 %reduce-scatter.2.cloned.1.call-done = f32[1024,256]{1,0:T(8,128)} async-done(((f32[1024,4096]{1,0:T(8,128)}), f32[1024,256]{1,0:T(8,128)}) %reduce-scatter.2.cloned.1.call-update) | async-done | bytes 1048592 | tf_op jit(solution)/shard_map/reduce_scatter | solution.py:74
  322.8 2.1 convert_element_type.24
  (7 shorter events, 0.1 us)
Async XLA Ops:
  8.2 33.9 %copy-start = (bf16[64,4096]{1,0:T(8,128)(2,1)S(1)}, bf16[64,4096]{1,0:T(8,128)(2,1)}, u32[]{:S(2)}) copy-start(bf16[64,4096]{1,0:T(8,128)(2,1)} %param.6) | copy-start | bytes 1572868
  43.6 42.9 %all-to-all-start = ((bf16[128,16,256]{2,1,0:T(8,128)(2,1)}), bf16[128,16,256]{2,1,0:T(8,128)(2,1)S(1)}, u32[]{:S(2)}, u32[]{:S(2)}) async-start(bf16[128,16,256]{2,1,0:T(8,128)(2,1)} %bitcast.7), calls=%async_computation | async-start | bytes 2097152 | tf_op jit(solution)/shard_map/all_to_all | solution.py:50
  55.1 115.4 %all-gather.2.cloned.1.call-start = ((), (), s32[]{:S(2)}) async-start(), calls=%async_computation.2 | async-start | bytes 8912896 | tf_op jit(solution)/shard_map/all_gather | solution.py:69
  91.5 231.3 %reduce-scatter.2.cloned.1.call-start = ((), (), s32[]{:S(2)}) async-start(), calls=%async_computation.3 | async-start | bytes 17825792 | tf_op jit(solution)/shard_map/reduce_scatter | solution.py:74
Sparse Core Ops, SparseCore 0:
  91.6 78.8 all-gather.1
  212.3 110.3 reduce-scatter.1
where the time goes:
time: 332 us
  waiting for transfers between devices  189 us (57%)
  local copies, waits for them, and re-layouts  68.5 us (21%)
  matrix products  43.2 us (13%)
  between operations  13.5 us (4%)
  starting transfers between devices  11.8 us (4%)
  other arithmetic  5.3 us (2%)
    reduce_scatter x1, waiting for transfers between devices, per_device(): lax.psum_scatter(partial_term, 'col', scatter_dimension=1, tiled=True)  111 us
    all_gather x1, waiting for transfers between devices, per_device(): piece = lax.all_gather(packed, 'col', axis=1, tiled=True)  78.7 us
    gather x5, local copies, waits for them, and re-layouts, destinations(): base = jnp.take_along_axis(offsets - starts, which, axis=1)  33.7 us
    scatter x1, local copies, waits for them, and re-layouts, per_device(): lookup = jnp.zeros((tok_row,), jnp.int32).at[landing.reshape(-1)].set(fla...  30.4 us
    dot_general x1, matrix products, per_device(): jnp.dot(hidden, down_weight, preferred_element_type=jnp.float32)  27.8 us
    dot_general x1, matrix products, per_device(): gate = jnp.dot(piece, gate_weight, preferred_element_type=jnp.float32)  14 us
    all_to_all x1, starting transfers between devices, per_device(): lax.all_to_all(outgoing.reshape(sources, capacity, col_width), ('row', 'c...  11.5 us
  transfers between devices with their start and end apart: 3, of which 2 were waited for; matrix products, arithmetic and copies ran while one was open for 9% of the time, Pallas kernels for 0%

commit v1 on v0

v1 whole, which is shorter than its diff:
```python
import functools

import jax
import jax.numpy as jnp
from jax import lax
from jax.experimental import pallas as pl
from jax.experimental.pallas import tpu as pltpu
from jax.sharding import PartitionSpec as P

MESH = pl.DeviceIdType.MESH
N_ROW = 8
N_COL = 16
RING = 4
LOAD = 64
CAP = 16
TRAJ = 8
TOK = 1024
HALF = 512
WIDTH = 256
SRC = N_ROW * N_COL
I32 = jnp.int32
F32 = jnp.float32
BF16 = jnp.bfloat16


def plan_kernel(len_s, off_s, len_t, off_t, loaded, out, table):
    row = lax.axis_index("row")
    me = row * N_COL + lax.axis_index("col")
    lane = lax.broadcasted_iota(I32, (LOAD, LOAD), 1)
    sub = lax.broadcasted_iota(I32, (LOAD, LOAD), 0)
    pos_l = jnp.zeros((LOAD, LOAD), I32)
    pos_s = jnp.zeros((LOAD, LOAD), I32)
    start = jnp.int32(0)
    for j in range(TRAJ):
        end = start + len_s[me, j]
        shift = off_s[me, j] - start
        pos_l = jnp.where((lane >= start) & (lane < end), shift + lane, pos_l)
        pos_s = jnp.where((sub >= start) & (sub < end), shift + sub, pos_s)
        start = end
    block_l = pos_l // TOK
    block_s = pos_s // TOK
    rank = jnp.sum(
        jnp.where((block_l == block_s) & (sub < lane), 1.0, 0.0), axis=0, keepdims=True
    ).astype(I32)
    target = block_l[0:1, :] * CAP + rank
    slot = lax.broadcasted_iota(I32, (N_ROW * CAP, LOAD), 0)
    select = jnp.where(target == slot, 1.0, 0.0).astype(BF16)
    for c in range(N_COL):
        picked = jnp.dot(select, loaded[:, c * WIDTH : (c + 1) * WIDTH], preferred_element_type=F32)
        out[:, c] = picked.astype(BF16).reshape(N_ROW, CAP, WIDTH)

    tok = lax.broadcasted_iota(I32, (LOAD, SRC), 0)
    pos = jnp.zeros((LOAD, SRC), I32)
    start = jnp.zeros((1, SRC), I32)
    for j in range(TRAJ):
        end = start + len_t[j : j + 1, :]
        pos = jnp.where((tok >= start) & (tok < end), off_t[j : j + 1, :] - start + tok, pos)
        start = end
    mine = pos // TOK == row
    below = jnp.where(sub > lane, 1.0, 0.0).astype(BF16)
    order = jnp.dot(below, jnp.where(mine, 1.0, 0.0).astype(BF16), preferred_element_type=F32)
    order = order.astype(I32)
    in_row = jnp.where(mine, pos % TOK + 1, 0)
    by_slot = jnp.concatenate(
        [
            jnp.sum(jnp.where(order == q, in_row, 0).astype(F32), axis=0, keepdims=True)
            for q in range(CAP)
        ],
        axis=0,
    ).astype(I32)
    wide_s = lax.broadcasted_iota(I32, (SRC, CAP), 0)
    wide_l = lax.broadcasted_iota(I32, (SRC, CAP), 1)
    spread = jnp.where(wide_s % CAP == wide_l, 1.0, 0.0).astype(BF16)
    sq_s = lax.broadcasted_iota(I32, (SRC, SRC), 0)
    sq_l = lax.broadcasted_iota(I32, (SRC, SRC), 1)
    keep = sq_l % 8 == sq_s // CAP
    group_s = lax.broadcasted_iota(I32, (CAP, SRC), 0)
    group_l = lax.broadcasted_iota(I32, (CAP, SRC), 1)
    group = jnp.where(group_l // 8 == group_s, 1.0, 0.0).astype(BF16)
    total = jnp.zeros((CAP, SRC), F32)
    for part, scale in ((by_slot // 32, 32.0), (by_slot % 32, 1.0)):
        y = jnp.dot(spread, part.astype(F32).astype(BF16), preferred_element_type=F32)
        y = jnp.where(keep, y, 0.0).astype(BF16)
        total = total + scale * lax.dot_general(
            group, y, (((1,), (1,)), ((), ())), preferred_element_type=F32
        )
    table[...] = total.astype(I32) - 1


def ffn_kernel(
    arrived, table, wg_hbm, wu_hbm, wd_hbm, out,
    wg, wu, wd, x, accg, accu, hid, hot, got,
    w_sem, ag_send, ag_recv, rs_send, rs_recv,
):
    row = lax.axis_index("row")
    col = lax.axis_index("col")
    swap = lax.rem(row, 2)
    cx = lax.div(col, RING)
    cy = lax.rem(col, RING)
    a0 = (1 - swap) * cx + swap * cy
    b0 = (1 - swap) * cy + swap * cx

    def col_of(da, db):
        a = lax.rem(a0 + da, RING)
        b = lax.rem(b0 + db, RING)
        return (1 - swap) * (a * RING + b) + swap * (b * RING + a)

    near = {
        "a+": (row, col_of(1, 0)),
        "a-": (row, col_of(3, 0)),
        "b+": (row, col_of(0, 1)),
        "b-": (row, col_of(0, 3)),
    }
    loads = [
        pltpu.make_async_copy(src, dst, w_sem.at[i])
        for i, (src, dst) in enumerate(((wg_hbm, wg), (wu_hbm, wu), (wd_hbm, wd)))
    ]
    for load in loads:
        load.start()

    barrier = pltpu.get_barrier_semaphore()
    for who in near.values():
        pl.semaphore_signal(barrier, inc=1, device_id=who, device_id_type=MESH)

    def compact(m):
        place = lax.broadcasted_iota(I32, (WIDTH, SRC), 0) + m * WIDTH
        for g in range(CAP):
            hot[:, g * SRC : (g + 1) * SRC] = jnp.where(
                table[g : g + 1, :] == place, 1.0, 0.0
            ).astype(BF16)
        x[0, m // 2, (m % 2) * WIDTH : (m % 2 + 1) * WIDTH, :] = jnp.dot(
            hot[...], arrived[...], preferred_element_type=F32
        ).astype(BF16)

    sends = {}
    count = [0]

    def forward(slot, h, way, to):
        copy = pltpu.make_async_remote_copy(
            src_ref=x.at[slot, h],
            dst_ref=x.at[to, h],
            send_sem=ag_send.at[count[0]],
            recv_sem=ag_recv.at[to, h],
            device_id=near[way],
            device_id_type=MESH,
        )
        count[0] += 1
        copy.start()
        sends.setdefault((slot, h), []).append(copy)

    def pass_on(slot, h):
        da, db = slot // RING, slot % RING
        if db == 0:
            if da == 0:
                forward(slot, h, "a-", 1 * RING)
                forward(slot, h, "a+", 3 * RING)
            if da == 3 and h == 0:
                forward(slot, h, "a+", 2 * RING)
            if da == 1 and h == 1:
                forward(slot, h, "a-", 2 * RING)
            forward(slot, h, "b-", da * RING + 1)
            forward(slot, h, "b+", da * RING + 3)
        if db == 3 and h == 0:
            forward(slot, h, "b+", da * RING + 2)
        if db == 1 and h == 1:
            forward(slot, h, "b-", da * RING + 2)

    def take(slot, h):
        pltpu.make_async_copy(x.at[slot, h], x.at[slot, h], ag_recv.at[slot, h]).wait()
        pass_on(slot, h)

    def gate_up(slots, first=False, last=False):
        ks = [
            pl.ds(pl.multiple_of(col_of(s // RING, s % RING) * WIDTH, WIDTH), WIDTH) for s in slots
        ]

        def chunk(m, carry):
            h = lax.div(m, 2)
            src = pl.ds(pl.multiple_of(lax.rem(m, 2) * WIDTH, WIDTH), WIDTH)
            dst = pl.ds(pl.multiple_of(m * WIDTH, WIDTH), WIDTH)
            g = u = None
            for s, k in zip(slots, ks):
                lhs = x[s, h, src, :]
                dg = jnp.dot(lhs, wg[k, :], preferred_element_type=F32)
                du = jnp.dot(lhs, wu[k, :], preferred_element_type=F32)
                g = dg if g is None else g + dg
                u = du if u is None else u + du
            if not first:
                g = accg[dst, :] + g
                u = accu[dst, :] + u
            if last:
                hid[dst, :] = (g / (1.0 + jnp.exp(-g)) * u).astype(BF16)
            else:
                accg[dst, :] = g
                accu[dst, :] = u
            return carry

        lax.fori_loop(0, TOK // WIDTH, chunk, 0)

    compact(0)
    compact(1)
    pl.semaphore_wait(barrier, 4)
    pass_on(0, 0)
    compact(2)
    compact(3)
    pass_on(0, 1)
    groups = [[4, 12], [1, 3], [8, 2], [5, 7], [13, 15], [6, 14], [9, 11], [10]]
    for load in loads[:2]:
        load.wait()
    pending = [0]
    for i, group in enumerate(groups):
        for slot in group:
            take(slot, 0)
            take(slot, 1)
        gate_up(pending, first=i == 0)
        pending = group
    gate_up(pending, last=True)
    loads[2].wait()

    spots = [(s, h) for s in (2, 6, 14, 10, 0, 1, 3, 4, 12, 5, 7, 13, 15, 8, 9, 11) for h in (0, 1)]
    started = []

    def product(slot, h):
        cols = pl.ds(pl.multiple_of(col_of(slot // RING, slot % RING) * WIDTH, WIDTH), WIDTH)
        return jnp.dot(
            hid[h * HALF : (h + 1) * HALF, :], wd[:, cols], preferred_element_type=F32
        )

    def landed(i):
        pltpu.make_async_copy(got.at[i], got.at[i], rs_recv.at[i]).wait()
        return got[i].astype(F32)

    def send(value, way, to):
        n = len(started)
        spot = spots[n]
        for copy in sends.pop(spot, []):
            copy.wait_send()
        x[spot[0], spot[1]] = value.astype(BF16)
        copy = pltpu.make_async_remote_copy(
            src_ref=x.at[spot[0], spot[1]],
            dst_ref=got.at[to],
            send_sem=rs_send.at[n],
            recv_sem=rs_recv.at[to],
            device_id=near[way],
            device_id_type=MESH,
        )
        copy.start()
        started.append(copy)

    def chain(da, h):
        return da * 2 + h

    def plus(da, h):
        return 8 + da * 2 + h

    def minus(da, h):
        return 16 + da * 2 + h

    def far(da):
        send(product(da * RING + 2, 0), "b-", chain(da, 0))
        send(product(da * RING + 2, 1), "b+", chain(da, 1))

    def direct(da):
        send(product(da * RING + 3, 1), "b-", plus(da, 1))
        send(product(da * RING + 1, 0), "b+", minus(da, 0))

    def middle(da):
        send(product(da * RING + 3, 0) + landed(chain(da, 0)), "b-", plus(da, 0))
        send(product(da * RING + 1, 1) + landed(chain(da, 1)), "b+", minus(da, 1))

    def total(da, h):
        return product(da * RING, h) + landed(plus(da, h)) + landed(minus(da, h))

    far(2)
    direct(2)
    far(1)
    middle(2)
    far(3)
    direct(1)
    direct(3)
    middle(1)
    far(0)
    middle(3)
    direct(0)
    send(total(2, 0), "a-", 24)
    send(total(2, 1), "a+", 25)
    middle(0)
    send(total(1, 0), "a+", 28)
    send(total(3, 1), "a-", 27)
    send(total(3, 0) + landed(24), "a-", 26)
    send(total(1, 1) + landed(25), "a+", 29)
    for h in (0, 1):
        out[h * HALF : (h + 1) * HALF, :] = (total(0, h) + landed(26 + h) + landed(28 + h)).astype(
            BF16
        )
    for copies in sends.values():
        for copy in copies:
            copy.wait_send()
    for copy in started:
        copy.wait_send()


def per_device(loaded, lengths, offsets, gate_weight, up_weight, down_weight):
    width, hidden = gate_weight.shape
    vmem = pl.BlockSpec(memory_space=pltpu.VMEM)
    smem = pl.BlockSpec(memory_space=pltpu.SMEM)
    hbm = pl.BlockSpec(memory_space=pl.ANY)
    outgoing, table = pl.pallas_call(
        plan_kernel,
        out_shape=(
            jax.ShapeDtypeStruct((N_ROW, N_COL, CAP, WIDTH), BF16),
            jax.ShapeDtypeStruct((CAP, SRC), I32),
        ),
        in_specs=[smem, smem, vmem, vmem, vmem],
        out_specs=(vmem, vmem),
        compiler_params=pltpu.CompilerParams(vmem_limit_bytes=32 * 1024 * 1024),
        name="plan",
    )(lengths, offsets, lengths.T, offsets.T, loaded)
    arrived = lax.all_to_all(
        outgoing.reshape(SRC, CAP, WIDTH), ("row", "col"), split_axis=0, concat_axis=0, tiled=True
    ).reshape(SRC * CAP, WIDTH)
    return pl.pallas_call(
        ffn_kernel,
        out_shape=jax.ShapeDtypeStruct((TOK, WIDTH), BF16),
        in_specs=[vmem, vmem, hbm, hbm, hbm],
        out_specs=vmem,
        scratch_shapes=[
            pltpu.VMEM((width, hidden), BF16),
            pltpu.VMEM((width, hidden), BF16),
            pltpu.VMEM((hidden, width), BF16),
            pltpu.VMEM((N_COL, 2, HALF, WIDTH), BF16),
            pltpu.VMEM((TOK, hidden), F32),
            pltpu.VMEM((TOK, hidden), F32),
            pltpu.VMEM((TOK, hidden), BF16),
            pltpu.VMEM((WIDTH, SRC * CAP), BF16),
            pltpu.VMEM((30, HALF, WIDTH), BF16),
            pltpu.SemaphoreType.DMA((3,)),
            pltpu.SemaphoreType.DMA((30,)),
            pltpu.SemaphoreType.DMA((N_COL, 2)),
            pltpu.SemaphoreType.DMA((30,)),
            pltpu.SemaphoreType.DMA((30,)),
        ],
        compiler_params=pltpu.CompilerParams(
            collective_id=0, has_side_effects=True, vmem_limit_bytes=60 * 1024 * 1024
        ),
        name="ffn",
    )(arrived, table, gate_weight, up_weight, down_weight)


def solution(mesh):
    placed = (P(("row", "col"), None), P(), P(), P(None, "col"), P(None, "col"), P("col", None))
    return jax.shard_map(
        per_device, mesh=mesh, in_specs=placed, out_specs=P("row", "col"), check_vma=False
    )
```

time: 332 us -> 157 us (0.47)
  waiting for transfers between devices: 189 us -> 0.01 us
  Pallas kernels: 0 us -> 114 us
  matrix products: 43.2 us -> 0 us
  local copies, waits for them, and re-layouts: 68.5 us -> 30.4 us
  between operations: 13.5 us -> 0.03 us
  other arithmetic: 5.3 us -> 0 us
    pallas_call x0 -> x2, Pallas kernels: none -> 114 us  [the longest x1 110 us: per_device(): pl.pallas_call(ffn_kernel, out_shape=jax.ShapeDtypeStruct((TOK, WIDTH), B...]
    reduce_scatter x1 -> x0, waiting for transfers between devices: 111 us -> none  [per_device(): lax.psum_scatter(partial_term, 'col', scatter_dimension=1, tiled=True)]
    all_gather x1 -> x0, waiting for transfers between devices: 78.7 us -> none  [per_device(): piece = lax.all_gather(packed, 'col', axis=1, tiled=True)]
    dot_general x3 -> x0, matrix products: 43.2 us -> none  [the longest x1 27.8 us: per_device(): jnp.dot(hidden, down_weight, preferred_element_type=jnp.float32)]
    gather x6 -> x0, local copies, waits for them, and re-layouts: 37.6 us -> none  [the longest x5 33.7 us: destinations(): base = jnp.take_along_axis(offsets - starts, which, axis=1)]
    scatter x1 -> x0, local copies, waits for them, and re-layouts: 30.4 us -> none  [per_device(): lookup = jnp.zeros((tok_row,), jnp.int32).at[landing.reshape(-1)].set(fla...]
    unnamed x2 -> x15, local copies, waits for them, and re-layouts: 0.01 us -> 30.4 us
  transfers between devices with their start and end apart: 3 -> 1, of which waited for: 2 -> 0; matrix products, arithmetic and copies ran while one was open for 9% -> 15% of each run, Pallas kernels for 0% -> 0%
where the time goes in v1:
time: 157 us; the launch traced here: 156 us
  Pallas kernels  114 us (73%)
  local copies, waits for them, and re-layouts  30.4 us (19%)
  starting transfers between devices  11.5 us (7%)
    pallas_call x1, Pallas kernels, per_device(): pl.pallas_call(ffn_kernel, out_shape=jax.ShapeDtypeStruct((TOK, WIDTH), B...  110 us
    unnamed x15, local copies, waits for them, and re-layouts  30.4 us
    all_to_all x1, starting transfers between devices, per_device(): lax.all_to_all(outgoing.reshape(SRC, CAP, WIDTH), ('row', 'col'), split_a...  11.5 us
    pallas_call x1, Pallas kernels, per_device(): pl.pallas_call(plan_kernel, out_shape=(jax.ShapeDtypeStruct((N_ROW, N_COL...  4.32 us
  transfers between devices with their start and end apart: 1, of which 0 were waited for; matrix products, arithmetic and copies ran while one was open for 15% of the time, Pallas kernels for 0%

profile of v1, /device:TPU:1, one launch (start us, length us, event | category | flops | bytes accessed | tf_op | source)
XLA Modules:
  0.0 156.0 jit_solution(11076975889557934681)
XLA Ops:
  0.0 0.8 copy.7.len_s
  0.8 0.8 copy.8.off_s
  1.6 0.0 copy-start
  1.6 1.0 copy-done
  2.6 0.0 copy-start.1
  2.6 0.7 copy-done.1
  3.3 0.0 copy-start.2
  3.3 0.7 copy-done.2
  4.0 4.3 %plan.1 = (bf16[8,16,16,256]{3,2,1,0:T(8,128)(2,1)}, s32[16,128]{1,0:T(8,128)S(1)}) custom-call(s32[128,8]{1,0:T(8,128)S(1)} %copy.7.len_s, s32[128,8]{1,0:T(8,128)S(1)} %copy.8.off_s, s32[8,128]{1,0:T(8,128)S(1)} %bitcast.4, s32[8,128]{1,0:T(8,128)S(1)} %bitcast.5, bf16[64,4096]{1,0:T(8,128)(2,1)S(1)} %copy-done), custom_call_target="tpu_custom_call" | custom-call | tf_op jit(solution)/shard_map/plan/pallas_call | solution.py:308
  8.3 0.0 copy-start.3
  8.3 0.6 copy-done.3
  8.9 11.5 %all-to-all-start = ((bf16[128,16,256]{2,1,0:T(8,128)(2,1)}), bf16[128,16,256]{2,1,0:T(8,128)(2,1)S(1)}, u32[]{:S(2)}, u32[]{:S(2)}) async-start(bf16[128,16,256]{2,1,0:T(8,128)(2,1)} %bitcast.2), calls=%async_computation | async-start | bytes 2097152 | tf_op jit(solution)/shard_map/all_to_all | solution.py:319
  20.4 11.7 %copy.9.wg_hbm = bf16[4096,924]{1,0:T(8,128)(2,1)} copy(bf16[4096,924]{0,1:T(8,128)(2,1)} %param.9) | data formatting | bytes 15138816 | tf_op args[3]
  32.2 11.2 %copy.10.wu_hbm = bf16[4096,924]{1,0:T(8,128)(2,1)} copy(bf16[4096,924]{0,1:T(8,128)(2,1)} %param.10) | data formatting | bytes 15138816 | tf_op args[4]
  43.4 0.0 all-to-all-done
  43.4 0.0 copy-start.4
  43.4 1.0 copy-done.4
  44.4 109.7 %ffn.1 = bf16[1024,256]{1,0:T(8,128)(2,1)} custom-call(bf16[2048,256]{1,0:T(8,128)(2,1)} %bitcast.6, s32[16,128]{1,0:T(8,128)} %copy-done.3, bf16[4096,924]{1,0:T(8,128)(2,1)} %copy.9.wg_hbm, bf16[4096,924]{1,0:T(8,128)(2,1)} %copy.10.wu_hbm, bf16[924,4096]{1,0:T(8,128)(2,1)} %wd_hbm.1), custom_call_target="tpu_custom_call" | custom-call | tf_op jit(solution)/shard_map/ffn/pallas_call | solution.py:322
  154.1 1.9 %copy.12 = bf16[1024,256]{1,0:T(8,128)(2,1)} copy(bf16[1024,256]{1,0:T(8,128)(2,1)} %ffn.1) | data formatting | bytes 1048576
Async XLA Ops:
  1.6 1.0 copy-start
  2.6 0.7 copy-start.1
  3.3 0.7 copy-start.2
  8.3 0.6 copy-start.3
  8.9 34.5 %all-to-all-start = ((bf16[128,16,256]{2,1,0:T(8,128)(2,1)}), bf16[128,16,256]{2,1,0:T(8,128)(2,1)S(1)}, u32[]{:S(2)}, u32[]{:S(2)}) async-start(bf16[128,16,256]{2,1,0:T(8,128)(2,1)} %bitcast.2), calls=%async_computation | async-start | bytes 2097152 | tf_op jit(solution)/shard_map/all_to_all | solution.py:319
  43.4 1.0 copy-start.4

commit v2 on v1

--- a/solution.py
+++ b/solution.py
@@ -18,22 +18,43 @@
 HALF = 512
 WIDTH = 256
 SRC = N_ROW * N_COL
+NT = (((1,), (1,)), ((), ()))
 I32 = jnp.int32
 F32 = jnp.float32
 BF16 = jnp.bfloat16
 
 
-def plan_kernel(len_s, off_s, len_t, off_t, loaded, out, table):
+def plan_kernel(len_t, off_t, loaded, arrived, table, out, local_sem, send_sem, recv_sem):
     row = lax.axis_index("row")
-    me = row * N_COL + lax.axis_index("col")
+    col = lax.axis_index("col")
+    me = row * N_COL + col
+    cx = lax.div(col, RING)
+    cy = lax.rem(col, RING)
+
+    def partner(k):
+        r = lax.rem(row + lax.div(k, N_COL), N_ROW)
+        x = lax.rem(cx + lax.rem(lax.div(k, RING), RING), RING)
+        y = lax.rem(cy + lax.rem(k, RING), RING)
+        return r, x * RING + y
+
+    barrier = pltpu.get_barrier_semaphore()
+
+    def greet(k, carry):
+        pl.semaphore_signal(barrier, inc=1, device_id=partner(k), device_id_type=MESH)
+        return carry
+
+    lax.fori_loop(1, SRC, greet, 0)
     lane = lax.broadcasted_iota(I32, (LOAD, LOAD), 1)
     sub = lax.broadcasted_iota(I32, (LOAD, LOAD), 0)
     pos_l = jnp.zeros((LOAD, LOAD), I32)
     pos_s = jnp.zeros((LOAD, LOAD), I32)
-    start = jnp.int32(0)
+    own = lax.broadcasted_iota(I32, (TRAJ, SRC), 1) == me
+    own_len = jnp.sum(jnp.where(own, len_t[...], 0).astype(F32), axis=1, keepdims=True).astype(I32)
+    own_off = jnp.sum(jnp.where(own, off_t[...], 0).astype(F32), axis=1, keepdims=True).astype(I32)
+    start = jnp.zeros((1, 1), I32)
     for j in range(TRAJ):
-        end = start + len_s[me, j]
-        shift = off_s[me, j] - start
+        end = start + own_len[j : j + 1, :]
+        shift = own_off[j : j + 1, :] - start
         pos_l = jnp.where((lane >= start) & (lane < end), shift + lane, pos_l)
         pos_s = jnp.where((sub >= start) & (sub < end), shift + sub, pos_s)
         start = end
@@ -48,6 +69,26 @@
     for c in range(N_COL):
         picked = jnp.dot(select, loaded[:, c * WIDTH : (c + 1) * WIDTH], preferred_element_type=F32)
         out[:, c] = picked.astype(BF16).reshape(N_ROW, CAP, WIDTH)
+    pl.semaphore_wait(barrier, SRC - 1)
+
+    def copy_to(k):
+        r, c = partner(k)
+        return pltpu.make_async_remote_copy(
+            src_ref=out.at[r, c],
+            dst_ref=arrived.at[me],
+            send_sem=send_sem,
+            recv_sem=recv_sem,
+            device_id=(r, c),
+            device_id_type=MESH,
+        )
+
+    def start(k, carry):
+        copy_to(k).start()
+        return carry
+
+    lax.fori_loop(1, SRC, start, 0)
+    own_copy = pltpu.make_async_copy(out.at[row, col], arrived.at[me], local_sem)
+    own_copy.start()
 
     tok = lax.broadcasted_iota(I32, (LOAD, SRC), 0)
     pos = jnp.zeros((LOAD, SRC), I32)
@@ -85,6 +126,10 @@
             group, y, (((1,), (1,)), ((), ())), preferred_element_type=F32
         )
     table[...] = total.astype(I32) - 1
+    own_copy.wait()
+    others = arrived.at[pl.ds(0, SRC - 1)]
+    pltpu.make_async_copy(others, others, recv_sem).wait()
+    pltpu.make_async_copy(others, others, send_sem).wait()
 
 
 def ffn_kernel(
@@ -181,8 +226,8 @@
             g = u = None
             for s, k in zip(slots, ks):
                 lhs = x[s, h, src, :]
-                dg = jnp.dot(lhs, wg[k, :], preferred_element_type=F32)
-                du = jnp.dot(lhs, wu[k, :], preferred_element_type=F32)
+                dg = lax.dot_general(lhs, wg[:, k], NT, preferred_element_type=F32)
+                du = lax.dot_general(lhs, wu[:, k], NT, preferred_element_type=F32)
                 g = dg if g is None else g + dg
                 u = du if u is None else u + du
             if not first:
@@ -303,30 +348,34 @@
 def per_device(loaded, lengths, offsets, gate_weight, up_weight, down_weight):
     width, hidden = gate_weight.shape
     vmem = pl.BlockSpec(memory_space=pltpu.VMEM)
-    smem = pl.BlockSpec(memory_space=pltpu.SMEM)
     hbm = pl.BlockSpec(memory_space=pl.ANY)
-    outgoing, table = pl.pallas_call(
+    arrived, table = pl.pallas_call(
         plan_kernel,
         out_shape=(
-            jax.ShapeDtypeStruct((N_ROW, N_COL, CAP, WIDTH), BF16),
+            jax.ShapeDtypeStruct((SRC, CAP, WIDTH), BF16),
             jax.ShapeDtypeStruct((CAP, SRC), I32),
         ),
-        in_specs=[smem, smem, vmem, vmem, vmem],
+        in_specs=[vmem, vmem, vmem],
         out_specs=(vmem, vmem),
-        compiler_params=pltpu.CompilerParams(vmem_limit_bytes=32 * 1024 * 1024),
-        name="plan",
-    )(lengths, offsets, lengths.T, offsets.T, loaded)
-    arrived = lax.all_to_all(
-        outgoing.reshape(SRC, CAP, WIDTH), ("row", "col"), split_axis=0, concat_axis=0, tiled=True
-    ).reshape(SRC * CAP, WIDTH)
+        scratch_shapes=[
+            pltpu.VMEM((N_ROW, N_COL, CAP, WIDTH), BF16),
+            pltpu.SemaphoreType.DMA,
+            pltpu.SemaphoreType.DMA,
+            pltpu.SemaphoreType.DMA,
+        ],
+        compiler_params=pltpu.CompilerParams(
+            collective_id=1, has_side_effects=True, vmem_limit_bytes=32 * 1024 * 1024
+        ),
+        name="dispatch",
+    )(lengths.T, offsets.T, loaded)
     return pl.pallas_call(
         ffn_kernel,
         out_shape=jax.ShapeDtypeStruct((TOK, WIDTH), BF16),
         in_specs=[vmem, vmem, hbm, hbm, hbm],
         out_specs=vmem,
         scratch_shapes=[
-            pltpu.VMEM((width, hidden), BF16),
-            pltpu.VMEM((width, hidden), BF16),
+            pltpu.VMEM((hidden, width), BF16),
+            pltpu.VMEM((hidden, width), BF16),
             pltpu.VMEM((hidden, width), BF16),
             pltpu.VMEM((N_COL, 2, HALF, WIDTH), BF16),
             pltpu.VMEM((TOK, hidden), F32),
@@ -344,7 +393,7 @@
             collective_id=0, has_side_effects=True, vmem_limit_bytes=60 * 1024 * 1024
         ),
         name="ffn",
-    )(arrived, table, gate_weight, up_weight, down_weight)
+    )(arrived.reshape(SRC * CAP, WIDTH), table, gate_weight.T, up_weight.T, down_weight)
 
 
 def solution(mesh):

time: 157 us -> 142 us (0.904)
  local copies, waits for them, and re-layouts: 30.4 us -> 5.85 us
  Pallas kernels: 114 us -> 136 us
  starting transfers between devices: 11.5 us -> 0 us
    unnamed x15 -> x11, local copies, waits for them, and re-layouts: 30.4 us -> 5.85 us
    pallas_call x1, Pallas kernels: 4.32 us -> 28.3 us  [per_device(): pl.pallas_call(plan_kernel, out_shape=(jax.ShapeDtypeStruct((SRC, CAP, WI...]
    all_to_all x1 -> x0, starting transfers between devices: 11.5 us -> none  [per_device(): lax.all_to_all(outgoing.reshape(SRC, CAP, WIDTH), ('row', 'col'), split_a...]
    pallas_call x1, Pallas kernels: 110 us -> 108 us  [per_device(): pl.pallas_call(ffn_kernel, out_shape=jax.ShapeDtypeStruct((TOK, WIDTH), B...]
  transfers between devices with their start and end apart: 1 -> 0, of which waited for: 0 -> 0; matrix products, arithmetic and copies ran while one was open for 15% -> 0% of each run, Pallas kernels for 0% -> 0%
where the time goes in v2:
time: 142 us
  Pallas kernels  136 us (96%)
  local copies, waits for them, and re-layouts  5.85 us (4%)
    pallas_call x1, Pallas kernels, per_device(): pl.pallas_call(ffn_kernel, out_shape=jax.ShapeDtypeStruct((TOK, WIDTH), B...  108 us
    pallas_call x1, Pallas kernels, per_device(): pl.pallas_call(plan_kernel, out_shape=(jax.ShapeDtypeStruct((SRC, CAP, WI...  28.3 us
    unnamed x11, local copies, waits for them, and re-layouts  5.85 us

profile of v2, /device:TPU:1, one launch (start us, length us, event | category | flops | bytes accessed | tf_op | source)
XLA Modules:
  0.0 142.2 jit_solution(9833556501006449421)
XLA Ops:
  0.0 0.0 copy-start.1
  0.0 1.0 copy-done.1
  1.0 0.0 copy-start.3
  1.0 0.7 copy-done.3
  1.7 0.0 copy-start.4
  1.7 0.7 copy-done.4
  2.4 28.3 %dispatch.1 = (bf16[128,16,256]{2,1,0:T(8,128)(2,1)S(1)}, s32[16,128]{1,0:T(8,128)S(1)}) custom-call(s32[8,128]{1,0:T(8,128)S(1)} %bitcast.6, s32[8,128]{1,0:T(8,128)S(1)} %bitcast.7, bf16[64,4096]{1,0:T(8,128)(2,1)S(1)} %copy-done.1), custom_call_target="tpu_custom_call" | custom-call | tf_op jit(solution)/shard_map/dispatch/pallas_call | solution.py:352
  30.7 0.0 copy-start
  30.7 1.0 copy-done
  31.7 0.0 copy-start.2
  31.7 0.6 copy-done.2
  32.3 108.0 %ffn.1 = bf16[1024,256]{1,0:T(8,128)(2,1)} custom-call(bf16[2048,256]{1,0:T(8,128)(2,1)} %bitcast.5, s32[16,128]{1,0:T(8,128)} %copy-done.2, bf16[924,4096]{1,0:T(8,128)(2,1)} %bitcast.8, bf16[924,4096]{1,0:T(8,128)(2,1)} %bitcast.9, bf16[924,4096]{1,0:T(8,128)(2,1)} %wd_hbm.1), custom_call_target="tpu_custom_call" | custom-call | tf_op jit(solution)/shard_map/ffn/pallas_call | solution.py:371
  140.3 1.9 %copy.8 = bf16[1024,256]{1,0:T(8,128)(2,1)} copy(bf16[1024,256]{1,0:T(8,128)(2,1)} %ffn.1) | data formatting | bytes 1048576
Async XLA Ops:
  0.0 1.0 copy-start.1
  1.0 0.7 copy-start.3
  1.7 0.7 copy-start.4
  30.7 1.0 copy-start
  31.7 0.6 copy-start.2
